TPU v7x, 512 devices: a whole 4x4x16 slice. The times are simulated.
512 devices in a mesh: row: 32 (over z_lo, y), col: 16 (over z_hi, x, core).
Axes of the slice: x: 4, y: 4, z: 16 (z_hi: 2, z_lo: 8; z = z_hi * 8 + z_lo), core: 2. Of those that a mesh axis runs over, the one named last changes fastest.
Arguments:
- entries: int32 [128, 64, 128, 128], P('row', 'col'), may hold values from -2 to 2
- tile_cols: int32 [128, 64], P('row', 'col'), may hold values from 0 to 31
- block_now: int32 [32, 65536], P(None, ('col', 'row')), may hold values from 0 to 65520
- block_prev: int32 [32, 65536], P(None, ('col', 'row')), may hold values from 0 to 65520
- block_prev2: int32 [32, 65536], P(None, ('col', 'row')), may hold values from 0 to 65520
- gram_prev: int32 [32, 32], replicated, may hold values from 0 to 65520
- square_prev: int32 [32, 32], replicated, may hold values from 0 to 65520
- inverse_prev: int32 [32, 32], replicated, may hold values from 0 to 65520
- inverse_prev2: int32 [32, 32], replicated, may hold values from 0 to 65520
Outputs:
- next_block: float32 [32, 65536], P(None, ('col', 'row'))
- later_block: float32 [32, 65536], P(None, ('col', 'row'))
Inputs may be any that keep to these rules, and one draw needn't show every extreme that they name: `tile_cols`: stored tiles that name the same tile column in one tile row add. `block_prev`: residues. `block_prev2`: residues. `gram_prev`: residues. `square_prev`: residues. `inverse_prev`: residues. `inverse_prev2`: residues.
All inputs are finite; a program needn't handle non-finite values.
Results may differ from a plain program's by a relative error of at most 0.0003.
Values sent between devices are 32-bit elements; how exact they have to be, the bound alone decides.
No kernel may reach another device: no remote copies, remote signals or barrier semaphores. Data moves between devices by JAX's collectives and lax.ppermute only.
A program may use at most 64 MiB of HBM per device.

v0:
```python
import jax
import jax.numpy as jnp
from jax import lax
from jax.sharding import PartitionSpec as P

modulus = 65521.0


def residue(values):
    return jnp.mod(values, modulus)


def split_digits(values):
    top_part = jnp.floor(values / 256.0)
    return (top_part, values - top_part * 256.0)


def fold_digits(top_sum, low_sum):
    return residue(residue(residue(top_sum) * 256.0) + residue(low_sum))


def fold_three(upper_part, middle, lower_part):
    return residue(
        residue(residue(upper_part) * 15.0) + residue(residue(middle) * 256.0) + residue(lower_part)
    )


def mulmod(left_side, right_side):
    top_part, low_part = split_digits(right_side)
    return fold_digits(left_side * top_part, left_side * low_part)


def exact_dot(left_side, right_side):
    return jnp.dot(
        left_side, right_side, precision=lax.Precision.HIGHEST, preferred_element_type=jnp.float32
    )


def small_product(left_side, right_side):
    left_top, left_low = split_digits(left_side)
    right_top, right_low = split_digits(right_side)
    return fold_three(
        exact_dot(left_top, right_top),
        exact_dot(left_top, right_low) + exact_dot(left_low, right_top),
        exact_dot(left_low, right_low),
    )


def inverse_scalar(number):
    result = jnp.ones_like(number)
    square = number
    exponent = 65519
    for position in range(16):
        if exponent >> position & 1:
            result = mulmod(result, square)
        square = mulmod(square, square)
    return result


def inverse_matrix(matrix):
    matrix_order = matrix.shape[0]
    augmented = jnp.concatenate([matrix, jnp.eye(matrix_order, dtype=matrix.dtype)], axis=1)
    row_numbers = jnp.arange(matrix_order, dtype=jnp.int32)

    def eliminate(column, augmented):
        column = jnp.asarray(column).astype(jnp.int32)
        pivot_column = augmented[:, column]
        usable = (pivot_column != 0.0) & (row_numbers >= column)
        pivot_row_id = jnp.where(jnp.any(usable), jnp.argmax(usable), column)
        pivot_row = augmented[pivot_row_id]
        current_row = augmented[column]
        swapped = jnp.where(
            (row_numbers == column)[:, None],
            pivot_row[None, :],
            jnp.where((row_numbers == pivot_row_id)[:, None], current_row[None, :], augmented),
        )
        scaled = mulmod(pivot_row, inverse_scalar(pivot_row[column]))
        factors = jnp.where(row_numbers == column, 0.0, swapped[:, column])
        reduced = residue(swapped - mulmod(factors[:, None], scaled[None, :]) + modulus)
        return jnp.where((row_numbers == column)[:, None], scaled[None, :], reduced)

    augmented = lax.fori_loop(0, matrix_order, eliminate, augmented)
    return augmented[:, matrix_order:]


def coefficients(
    gram_now, square_now, inverse_now, inverse_prev, inverse_prev2, gram_old, square_old
):
    identity = jnp.eye(gram_now.shape[0], dtype=gram_now.dtype)
    first = residue(identity - small_product(residue(square_now + gram_now), inverse_now) + modulus)
    second = residue(modulus - small_product(gram_now, inverse_prev))
    middle = residue(identity - small_product(inverse_prev, gram_old) + modulus)
    third = residue(
        modulus
        - small_product(small_product(residue(square_old + gram_old), middle), inverse_prev2)
    )
    return jnp.concatenate([first, second, third], axis=1)


def digit_stack(values):
    top_part, low_part = split_digits(values)
    return jnp.stack([top_part, low_part]).astype(jnp.bfloat16)


def combine_blocks(coeffs, stacked):
    products = jnp.einsum(
        "dab,ebn->dean",
        digit_stack(coeffs),
        digit_stack(stacked),
        preferred_element_type=jnp.float32,
    )
    return fold_three(products[0, 0], products[0, 1] + products[1, 0], products[1, 1])


def gram_local(first, second):
    column_count = first.shape[1]
    group_width = min(column_count, 128)
    groups = column_count // group_width
    first_digits = digit_stack(first).reshape(2, first.shape[0], groups, group_width)
    second_digits = digit_stack(second).reshape(2, second.shape[0], groups, group_width)
    products = jnp.einsum(
        "dagw,ecgw->gdeac", first_digits, second_digits, preferred_element_type=jnp.float32
    )
    per_group = fold_three(
        products[:, 0, 0], products[:, 0, 1] + products[:, 1, 0], products[:, 1, 1]
    )
    return residue(jnp.sum(per_group, axis=0))


def digit_pair(values):
    top_part, low_part = split_digits(values)
    return jnp.stack([top_part, low_part])


def forward_partial(block_full, tile_values, tile_cols):
    tile_rows, slot_count, tile_size = (
        tile_values.shape[0],
        tile_values.shape[1],
        tile_values.shape[2],
    )
    block_rows = block_full.shape[0]
    top_part, low_part = split_digits(block_full)
    digits = jnp.concatenate([top_part, low_part], axis=0).astype(jnp.bfloat16)
    digits = digits.reshape(2 * block_rows, -1, tile_size)
    picked = jnp.take(digits, tile_cols.reshape(-1), axis=1).reshape(
        2 * block_rows, tile_rows, slot_count, tile_size
    )
    raw_sums = jnp.einsum("brsk,rsjk->brj", picked, tile_values, preferred_element_type=jnp.float32)
    return fold_digits(raw_sums[:block_rows], raw_sums[block_rows:]).reshape(
        block_rows, tile_rows * tile_size
    )


def backward_partial(projected, tile_values, onehot):
    tile_rows, tile_size = (tile_values.shape[0], tile_values.shape[2])
    block_rows = projected.shape[0]
    top_part, low_part = split_digits(projected)
    digits = (
        jnp.concatenate([top_part, low_part], axis=0)
        .astype(jnp.bfloat16)
        .reshape(2 * block_rows, tile_rows, tile_size)
    )
    spread = jnp.einsum("brj,rsjk->brsk", digits, tile_values, preferred_element_type=jnp.float32)
    raw_sums = jnp.einsum(
        "brsk,rsc->bck",
        spread,
        onehot,
        precision=lax.Precision.HIGHEST,
        preferred_element_type=jnp.float32,
    )
    return fold_digits(raw_sums[:block_rows], raw_sums[block_rows:]).reshape(block_rows, -1)


def body(
    entries,
    tile_cols,
    block_now,
    block_prev,
    block_prev2,
    gram_prev,
    square_prev,
    inverse_prev,
    inverse_prev2,
):
    tile_values = entries.astype(jnp.bfloat16)
    tile_size = tile_values.shape[2]
    share_width = block_now.shape[1]
    col_tiles = share_width * lax.axis_size("row") // tile_size
    onehot = (
        tile_cols[:, :, None] == jnp.arange(col_tiles, dtype=jnp.int32)[None, None, :]
    ).astype(jnp.float32)
    current = block_now.astype(jnp.float32)
    earlier = block_prev.astype(jnp.float32)
    earliest = block_prev2.astype(jnp.float32)
    gram_old = gram_prev.astype(jnp.float32)
    square_old = square_prev.astype(jnp.float32)
    inverse_old = inverse_prev.astype(jnp.float32)
    inverse_older = inverse_prev2.astype(jnp.float32)
    results = []
    for iteration in range(2):
        block_full = lax.all_gather(current, "row", axis=1, tiled=True)
        projected = residue(lax.psum(forward_partial(block_full, tile_values, tile_cols), "col"))
        partial_term = backward_partial(projected, tile_values, onehot)
        applied = residue(lax.psum_scatter(partial_term, "row", scatter_dimension=1, tiled=True))
        current_own = current
        both_sums = lax.psum(
            jnp.stack(
                [
                    digit_pair(gram_local(current_own, applied)),
                    digit_pair(gram_local(applied, applied)),
                ]
            ),
            ("row", "col"),
        )
        gram_now = fold_digits(both_sums[0, 0], both_sums[0, 1])
        square_now = fold_digits(both_sums[1, 0], both_sums[1, 1])
        inverse_now = inverse_matrix(gram_now)
        coeffs = coefficients(
            gram_now, square_now, inverse_now, inverse_old, inverse_older, gram_old, square_old
        )
        stacked = jnp.concatenate([current, earlier, earliest], axis=0)
        following = residue(applied + combine_blocks(coeffs, stacked))
        results.append(following / modulus)
        earliest, earlier, current = (earlier, current, following)
        inverse_older, inverse_old = (inverse_old, inverse_now)
        gram_old, square_old = (gram_now, square_now)
    return (results[0], results[1])


def solution(mesh):
    placed = (
        P("row", "col", None, None),
        P("row", "col"),
        P(None, ("col", "row")),
        P(None, ("col", "row")),
        P(None, ("col", "row")),
        P(),
        P(),
        P(),
        P(),
    )
    return jax.shard_map(
        body,
        mesh=mesh,
        in_specs=placed,
        out_specs=(P(None, ("col", "row")), P(None, ("col", "row"))),
        check_vma=False,
    )
```

profile of v0, /device:TPU:1, one launch (start us, length us, event | category | flops | bytes accessed | tf_op | source)
XLA Modules:
  0.0 2244.6 jit_solution(948067549384732013)
XLA Ops:
  7.2 0.8 reshape.1652
  8.8 114.7 %all_gather.6 = f32[32,4096]{1,0:T(8,128)S(1)} all-gather(f32[32,128]{1,0:T(8,128)S(1)} %get-tuple-element.319), channel_id=1, replica_groups=mesh['row'=32,'col'=16] {'row'}, dimensions={1}, use_global_device_ids=true | all-gather | bytes 540672 | tf_op jit(solution)/shard_map/all_gather | solution.py:201
  124.9 0.8 copy_bitcast_fusion.7
  129.3 247.2 %all-reduce.3.cloned.1.call-done = f32[32,512]{1,0:T(8,128)} async-done(((f32[32,512]{1,0:T(8,128)}), f32[32,512]{1,0:T(8,128)}) %all-reduce.3.cloned.1.call-update) | async-done | bytes 65552 | tf_op jit(solution)/shard_map/psum | solution.py:202
  376.5 0.9 fusion.102
  378.1 1.1 convolution_bitcast_fusion.1
  379.2 1.1 add_select_fusion.22
  380.3 1.1 copy.355
  383.5 212.7 %reduce-scatter.3.cloned.1.call-done = f32[32,128]{1,0:T(8,128)} async-done(((f32[32,4096]{1,0:T(8,128)}), f32[32,128]{1,0:T(8,128)}) %reduce-scatter.3.cloned.1.call-update) | async-done | bytes 16400 | tf_op jit(solution)/shard_map/reduce_scatter | solution.py:204
  596.2 0.7 fusion.339
  597.5 125.4 %psum.29 = f32[2,2,32,32]{2,3,1,0:T(8,128)S(1)} all-reduce(f32[2,2,32,32]{2,3,1,0:T(8,128)S(1)} %pad_maximum_fusion.2), channel_id=1, replica_groups=mesh['row'=32,'col'=16] {'row','col'}, use_global_device_ids=true, to_apply=%region_2.4 | all-reduce | flops 4096 | bytes 32768 | tf_op jit(solution)/shard_map/psum | solution.py:206
  722.9 403.5 %while.36 = (s32[]{:T(128)}, f32[32,64]{0,1:T(8,128)S(1)}, s32[]{:T(128)}, s32[]{:T(128)}, s32[]{:T(128)}, /*index=5*/s32[]{:T(128)}, s32[]{:T(128)}, f32[]{:T(128)}, f32[]{:T(128)}, f32[]{:T(128)}, /*index=10*/f32[]{:T(128)}) while((s32[]{:T(128)}, f32[32,64]{0,1:T(8,128)S(1)}, s32[]{:T(128)}, s32[]{:T(128)}, ...), condition=%wide.region_6.8_spmd.clone.clone, body=%wide.region_3.7_spmd.clone.clone.sunk | while | flops 87498 | bytes 50118 | solution.py:82
  723.6 0.7 iota_reduce_fusion.4
  736.2 0.7 iota_reduce_fusion.4
  761.4 0.7 iota_reduce_fusion.4
  799.3 0.7 iota_reduce_fusion.4
  837.1 0.7 iota_reduce_fusion.4
  862.3 0.7 iota_reduce_fusion.4
  874.9 0.7 iota_reduce_fusion.4
  900.1 0.7 iota_reduce_fusion.4
  938.0 0.7 iota_reduce_fusion.4
  963.2 0.7 iota_reduce_fusion.4
  975.8 0.7 iota_reduce_fusion.4
  1001.0 0.7 iota_reduce_fusion.4
  1038.8 0.7 iota_reduce_fusion.4
  1076.7 0.7 iota_reduce_fusion.4
  1101.9 0.7 iota_reduce_fusion.4
  1114.5 0.7 iota_reduce_fusion.4
  1129.8 103.1 %all_gather.7 = f32[32,4096]{1,0:T(8,128)S(1)} all-gather(f32[32,128]{1,0:T(8,128)S(1)} %get-tuple-element.280), channel_id=1, replica_groups=mesh['row'=32,'col'=16] {'row'}, dimensions={1}, use_global_device_ids=true | all-gather | bytes 540672 | tf_op jit(solution)/shard_map/all_gather | solution.py:201
  1234.2 0.8 copy_bitcast_fusion.6
  1235.6 249.9 %all-reduce.5.cloned.1.call-done = f32[32,512]{1,0:T(8,128)} async-done(((f32[32,512]{1,0:T(8,128)}), f32[32,512]{1,0:T(8,128)}) %all-reduce.5.cloned.1.call-update) | async-done | bytes 65552 | tf_op jit(solution)/shard_map/psum | solution.py:202
  1485.5 0.9 fusion.103
  1486.7 1.1 convolution_bitcast_fusion
  1487.7 1.1 add_select_fusion.18
  1488.9 1.1 copy.354
  1491.4 213.1 %reduce-scatter.5.cloned.1.call-done = f32[32,128]{1,0:T(8,128)} async-done(((f32[32,4096]{1,0:T(8,128)}), f32[32,128]{1,0:T(8,128)}) %reduce-scatter.5.cloned.1.call-update) | async-done | bytes 16400 | tf_op jit(solution)/shard_map/reduce_scatter | solution.py:204
  1704.5 0.7 fusion.343
  1705.8 125.7 %psum.31 = f32[2,2,32,32]{2,3,1,0:T(8,128)S(1)} all-reduce(f32[2,2,32,32]{2,3,1,0:T(8,128)S(1)} %pad_maximum_fusion.3), channel_id=1, replica_groups=mesh['row'=32,'col'=16] {'row','col'}, use_global_device_ids=true, to_apply=%region_9.11 | all-reduce | flops 4096 | bytes 32768 | tf_op jit(solution)/shard_map/psum | solution.py:206
  1831.6 403.5 %while.37 = (s32[]{:T(128)}, f32[32,64]{0,1:T(8,128)S(1)}, s32[]{:T(128)}, s32[]{:T(128)}, s32[]{:T(128)}, /*index=5*/s32[]{:T(128)}, s32[]{:T(128)}, f32[]{:T(128)}, f32[]{:T(128)}, f32[]{:T(128)}, /*index=10*/f32[]{:T(128)}) while((s32[]{:T(128)}, f32[32,64]{0,1:T(8,128)S(1)}, s32[]{:T(128)}, s32[]{:T(128)}, ...), condition=%wide.region_13.15_spmd.clone.clone, body=%wide.region_10.14_spmd.clone.clone.sunk | while | flops 87498 | bytes 50118 | solution.py:82
  1832.2 0.7 iota_reduce_fusion.5
  1844.8 0.7 iota_reduce_fusion.5
  1983.5 0.7 iota_reduce_fusion.5
  1996.1 0.7 iota_reduce_fusion.5
  2008.8 0.7 iota_reduce_fusion.5
  2021.4 0.7 iota_reduce_fusion.5
  2034.0 0.7 iota_reduce_fusion.5
  2046.6 0.7 iota_reduce_fusion.5
  2059.2 0.7 iota_reduce_fusion.5
  (690 shorter events, 167.3 us)
Async XLA Ops:
  7.2 116.5 %copy-start = (s32[4,4,128,128]{3,2,1,0:T(8,128)S(1)}, s32[4,4,128,128]{3,2,1,0:T(8,128)}, u32[]{:S(2)}) copy-start(s32[4,4,128,128]{3,2,1,0:T(8,128)} %param.15) | copy-start | bytes 3145732
  7.2 369.3 %all-reduce.3.cloned.1.call-start = ((), (), s32[]{:S(2)}) async-start(), calls=%async_computation.2 | async-start | bytes 131072 | tf_op jit(solution)/shard_map/psum | solution.py:202
  125.7 0.7 copy-start.5
  125.7 0.8 copy-start.6
  125.7 470.4 %reduce-scatter.3.cloned.1.call-start = ((), (), s32[]{:S(2)}) async-start(), calls=%async_computation.3 | async-start | bytes 540672 | tf_op jit(solution)/shard_map/reduce_scatter | solution.py:204
  126.9 0.7 copy-start.7
  128.2 0.7 copy-start.8
  377.4 0.7 copy-start.4
  381.5 1104.0 %all-reduce.5.cloned.1.call-start = ((), (), s32[]{:S(2)}) async-start(), calls=%async_computation.4 | async-start | bytes 131072 | tf_op jit(solution)/shard_map/psum | solution.py:202
  382.0 0.7 copy-start.9
  382.0 0.7 copy-start.10
  382.8 0.7 copy-start.1
  1129.0 0.7 copy-start.2
  1235.0 469.5 %reduce-scatter.5.cloned.1.call-start = ((), (), s32[]{:S(2)}) async-start(), calls=%async_computation.5 | async-start | bytes 540672 | tf_op jit(solution)/shard_map/reduce_scatter | solution.py:204
  2236.6 0.7 copy-start.3
Sparse Core Ops, SparseCore 0:
  125.8 250.6 all-reduce.2
  381.6 214.5 reduce-scatter.2
  1235.1 250.3 all-reduce.4
  1490.1 214.3 reduce-scatter.4
where the time goes:
time: 2250 us; the launch traced here: 2240 us
  waiting for transfers between devices  923 us (41%)
  loops' own time  641 us (28%)
  blocking collectives  469 us (21%)
  other arithmetic  139 us (6%)
  local copies, waits for them, and re-layouts  47.5 us (2%)
    another operation x2, loops' own time, inverse_matrix(): augmented = lax.fori_loop(0, matrix_order, eliminate, augmented)  641 us
    psum x2, waiting for transfers between devices, body(): lax.psum(forward_partial(block_full, tile_values, tile_cols), 'col')  497 us
    reduce_scatter x2, waiting for transfers between devices, body(): lax.psum_scatter(partial_term, 'row', scatter_dimension=1, tiled=True)  426 us
    psum x2, blocking collectives, body(): lax.psum(jnp.stack([digit_pair(gram_local(current_own, applied)), digit_p...  251 us
    all_gather x2, blocking collectives, body(): block_full = lax.all_gather(current, 'row', axis=1, tiled=True)  218 us
    another operation x64, other arithmetic, eliminate(): pivot_row_id = jnp.where(jnp.any(usable), jnp.argmax(usable), column)  46.5 us
  transfers between devices with their start and end apart: 4, of which 4 were waited for; matrix products, arithmetic and copies ran while one was open for 0% of the time, Pallas kernels for 0%

commit v1 on v0

--- a/solution.py
+++ b/solution.py
@@ -4,6 +4,11 @@
 from jax.sharding import PartitionSpec as P
 
 modulus = 65521.0
+
+
+def outputs_state(sample, link_axis, which_axis):
+    extra = jax.lax.psum(sample, axis_name=link_axis)
+    return jax.lax.psum(extra, axis_name=which_axis)
 
 
 def residue(values):
@@ -203,14 +208,15 @@
         partial_term = backward_partial(projected, tile_values, onehot)
         applied = residue(lax.psum_scatter(partial_term, "row", scatter_dimension=1, tiled=True))
         current_own = current
-        both_sums = lax.psum(
+        both_sums = outputs_state(
             jnp.stack(
                 [
                     digit_pair(gram_local(current_own, applied)),
                     digit_pair(gram_local(applied, applied)),
                 ]
             ),
-            ("row", "col"),
+            "row",
+            which_axis="col",
         )
         gram_now = fold_digits(both_sums[0, 0], both_sums[0, 1])
         square_now = fold_digits(both_sums[1, 0], both_sums[1, 1])

time: 2250 us -> 2740 us (1.22)
  blocking collectives: 469 us -> 936 us
    psum x2 -> x4, blocking collectives: 251 us -> 721 us  [the longest x2 394 us: outputs_state(): extra = jax.lax.psum(sample, axis_name=link_axis)]
where the time goes in v1:
time: 2740 us; the launch traced here: 2730 us
  waiting for transfers between devices  939 us (34%)
  blocking collectives  936 us (34%)
  loops' own time  641 us (23%)
  other arithmetic  139 us (5%)
  local copies, waits for them, and re-layouts  47.5 us (2%)
    another operation x2, loops' own time, inverse_matrix(): augmented = lax.fori_loop(0, matrix_order, eliminate, augmented)  641 us
    psum x2, waiting for transfers between devices, body(): lax.psum(forward_partial(block_full, tile_values, tile_cols), 'col')  513 us
    reduce_scatter x2, waiting for transfers between devices, body(): lax.psum_scatter(partial_term, 'row', scatter_dimension=1, tiled=True)  426 us
    psum x2, blocking collectives, outputs_state(): extra = jax.lax.psum(sample, axis_name=link_axis)  394 us
    psum x2, blocking collectives, outputs_state(): return jax.lax.psum(extra, axis_name=which_axis)  327 us
    all_gather x2, blocking collectives, body(): block_full = lax.all_gather(current, 'row', axis=1, tiled=True)  215 us
  transfers between devices with their start and end apart: 4, of which 4 were waited for; matrix products, arithmetic and copies ran while one was open for 0% of the time, Pallas kernels for 0%

profile of v1, /device:TPU:1, one launch (start us, length us, event | category | flops | bytes accessed | tf_op | source)
XLA Modules:
  0.0 2727.5 jit_solution(17191804199030291254)
XLA Ops:
  7.2 0.8 reshape.1652
  8.8 114.7 %all_gather.6 = f32[32,4096]{1,0:T(8,128)S(1)} all-gather(f32[32,128]{1,0:T(8,128)S(1)} %get-tuple-element.319), channel_id=1, replica_groups=mesh['row'=32,'col'=16] {'row'}, dimensions={1}, use_global_device_ids=true | all-gather | bytes 540672 | tf_op jit(solution)/shard_map/all_gather | solution.py:206
  124.9 0.8 copy_bitcast_fusion.7
  129.3 247.2 %all-reduce.3.cloned.1.call-done = f32[32,512]{1,0:T(8,128)} async-done(((f32[32,512]{1,0:T(8,128)}), f32[32,512]{1,0:T(8,128)}) %all-reduce.3.cloned.1.call-update) | async-done | bytes 65552 | tf_op jit(solution)/shard_map/psum | solution.py:207
  376.5 0.9 fusion.102
  378.1 1.1 convolution_bitcast_fusion.1
  379.2 1.1 add_select_fusion.22
  380.3 1.1 copy.355
  383.5 212.7 %reduce-scatter.3.cloned.1.call-done = f32[32,128]{1,0:T(8,128)} async-done(((f32[32,4096]{1,0:T(8,128)}), f32[32,128]{1,0:T(8,128)}) %reduce-scatter.3.cloned.1.call-update) | async-done | bytes 16400 | tf_op jit(solution)/shard_map/reduce_scatter | solution.py:209
  596.2 0.7 fusion.339
  597.5 196.9 %psum.43 = f32[2,2,32,32]{2,3,1,0:T(8,128)S(1)} all-reduce(f32[2,2,32,32]{2,3,1,0:T(8,128)S(1)} %pad_maximum_fusion.2), channel_id=1, replica_groups=mesh['row'=32,'col'=16] {'row'}, use_global_device_ids=true, to_apply=%region_2.4 | all-reduce | flops 4096 | bytes 32768 | tf_op jit(solution)/shard_map/psum | solution.py:10
  794.4 163.6 %psum.44 = f32[2,2,32,32]{2,3,1,0:T(8,128)S(1)} all-reduce(f32[2,2,32,32]{2,3,1,0:T(8,128)S(1)} %psum.43), channel_id=1, replica_groups=mesh['row'=32,'col'=16] {'col'}, use_global_device_ids=true, to_apply=%region_3.5 | all-reduce | flops 4096 | bytes 32768 | tf_op jit(solution)/shard_map/psum | solution.py:11
  958.0 403.5 %while.36 = (s32[]{:T(128)}, f32[32,64]{0,1:T(8,128)S(1)}, s32[]{:T(128)}, s32[]{:T(128)}, s32[]{:T(128)}, /*index=5*/s32[]{:T(128)}, s32[]{:T(128)}, f32[]{:T(128)}, f32[]{:T(128)}, f32[]{:T(128)}, /*index=10*/f32[]{:T(128)}) while((s32[]{:T(128)}, f32[32,64]{0,1:T(8,128)S(1)}, s32[]{:T(128)}, s32[]{:T(128)}, ...), condition=%wide.region_7.9_spmd.clone.clone, body=%wide.region_4.8_spmd.clone.clone.sunk | while | flops 87498 | bytes 50118 | solution.py:87
  958.7 0.7 iota_reduce_fusion.4
  971.3 0.7 iota_reduce_fusion.4
  983.9 0.7 iota_reduce_fusion.4
  996.5 0.7 iota_reduce_fusion.4
  1009.1 0.7 iota_reduce_fusion.4
  1021.7 0.7 iota_reduce_fusion.4
  1034.4 0.7 iota_reduce_fusion.4
  1173.0 0.7 iota_reduce_fusion.4
  1185.7 0.7 iota_reduce_fusion.4
  1198.3 0.7 iota_reduce_fusion.4
  1210.9 0.7 iota_reduce_fusion.4
  1223.5 0.7 iota_reduce_fusion.4
  1236.1 0.7 iota_reduce_fusion.4
  1248.7 0.7 iota_reduce_fusion.4
  1261.3 0.7 iota_reduce_fusion.4
  1273.9 0.7 iota_reduce_fusion.4
  1364.9 100.5 %all_gather.7 = f32[32,4096]{1,0:T(8,128)S(1)} all-gather(f32[32,128]{1,0:T(8,128)S(1)} %get-tuple-element.280), channel_id=1, replica_groups=mesh['row'=32,'col'=16] {'row'}, dimensions={1}, use_global_device_ids=true | all-gather | bytes 540672 | tf_op jit(solution)/shard_map/all_gather | solution.py:206
  1466.7 0.8 copy_bitcast_fusion.6
  1468.0 265.4 %all-reduce.5.cloned.1.call-done = f32[32,512]{1,0:T(8,128)} async-done(((f32[32,512]{1,0:T(8,128)}), f32[32,512]{1,0:T(8,128)}) %all-reduce.5.cloned.1.call-update) | async-done | bytes 65552 | tf_op jit(solution)/shard_map/psum | solution.py:207
  1733.5 0.9 fusion.103
  1734.6 1.1 convolution_bitcast_fusion
  1735.7 1.1 add_select_fusion.18
  1736.8 1.1 copy.354
  1739.3 213.3 %reduce-scatter.5.cloned.1.call-done = f32[32,128]{1,0:T(8,128)} async-done(((f32[32,4096]{1,0:T(8,128)}), f32[32,128]{1,0:T(8,128)}) %reduce-scatter.5.cloned.1.call-update) | async-done | bytes 16400 | tf_op jit(solution)/shard_map/reduce_scatter | solution.py:209
  1952.6 0.7 fusion.343
  1953.9 196.9 %psum.46 = f32[2,2,32,32]{2,3,1,0:T(8,128)S(1)} all-reduce(f32[2,2,32,32]{2,3,1,0:T(8,128)S(1)} %pad_maximum_fusion.3), channel_id=1, replica_groups=mesh['row'=32,'col'=16] {'row'}, use_global_device_ids=true, to_apply=%region_10.12 | all-reduce | flops 4096 | bytes 32768 | tf_op jit(solution)/shard_map/psum | solution.py:10
  2150.8 163.6 %psum.47 = f32[2,2,32,32]{2,3,1,0:T(8,128)S(1)} all-reduce(f32[2,2,32,32]{2,3,1,0:T(8,128)S(1)} %psum.46), channel_id=1, replica_groups=mesh['row'=32,'col'=16] {'col'}, use_global_device_ids=true, to_apply=%region_11.13 | all-reduce | flops 4096 | bytes 32768 | tf_op jit(solution)/shard_map/psum | solution.py:11
  2314.5 403.5 %while.37 = (s32[]{:T(128)}, f32[32,64]{0,1:T(8,128)S(1)}, s32[]{:T(128)}, s32[]{:T(128)}, s32[]{:T(128)}, /*index=5*/s32[]{:T(128)}, s32[]{:T(128)}, f32[]{:T(128)}, f32[]{:T(128)}, f32[]{:T(128)}, /*index=10*/f32[]{:T(128)}) while((s32[]{:T(128)}, f32[32,64]{0,1:T(8,128)S(1)}, s32[]{:T(128)}, s32[]{:T(128)}, ...), condition=%wide.region_15.17_spmd.clone.clone, body=%wide.region_12.16_spmd.clone.clone.sunk | while | flops 87498 | bytes 50118 | solution.py:87
  2315.2 0.7 iota_reduce_fusion.5
  2327.8 0.7 iota_reduce_fusion.5
  2340.4 0.7 iota_reduce_fusion.5
  2353.0 0.7 iota_reduce_fusion.5
  2365.6 0.7 iota_reduce_fusion.5
  2378.2 0.7 iota_reduce_fusion.5
  2390.8 0.7 iota_reduce_fusion.5
  (692 shorter events, 168.7 us)
Async XLA Ops:
  7.2 116.5 %copy-start = (s32[4,4,128,128]{3,2,1,0:T(8,128)S(1)}, s32[4,4,128,128]{3,2,1,0:T(8,128)}, u32[]{:S(2)}) copy-start(s32[4,4,128,128]{3,2,1,0:T(8,128)} %param.15) | copy-start | bytes 3145732
  7.2 369.3 %all-reduce.3.cloned.1.call-start = ((), (), s32[]{:S(2)}) async-start(), calls=%async_computation.2 | async-start | bytes 131072 | tf_op jit(solution)/shard_map/psum | solution.py:207
  125.7 0.7 copy-start.5
  125.7 0.8 copy-start.6
  125.7 470.4 %reduce-scatter.3.cloned.1.call-start = ((), (), s32[]{:S(2)}) async-start(), calls=%async_computation.3 | async-start | bytes 540672 | tf_op jit(solution)/shard_map/reduce_scatter | solution.py:209
  126.9 0.7 copy-start.7
  128.2 0.7 copy-start.8
  377.4 0.7 copy-start.4
  381.5 1352.0 %all-reduce.5.cloned.1.call-start = ((), (), s32[]{:S(2)}) async-start(), calls=%async_computation.4 | async-start | bytes 131072 | tf_op jit(solution)/shard_map/psum | solution.py:207
  382.0 0.7 copy-start.9
  382.0 0.7 copy-start.10
  382.8 0.7 copy-start.1
  1364.1 0.7 copy-start.2
  1467.5 485.1 %reduce-scatter.5.cloned.1.call-start = ((), (), s32[]{:S(2)}) async-start(), calls=%async_computation.5 | async-start | bytes 540672 | tf_op jit(solution)/shard_map/reduce_scatter | solution.py:209
  2719.6 0.7 copy-start.3
Sparse Core Ops, SparseCore 0:
  125.8 250.6 all-reduce.2
  381.6 214.5 reduce-scatter.2
  1467.6 265.8 all-reduce.4
  1738.1 214.5 reduce-scatter.4
